TPU v7x, 128 devices: a whole 4x4x4 slice. The times are simulated.
128 devices in a mesh: rep: 4 (over z), emb: 32 (over y, x, core).
Axes of the slice: x: 4, y: 4, z: 4, core: 2. Of those that a mesh axis runs over, the one named last changes fastest.
Arguments:
- tables: bfloat16 [800, 1024, 128], P('emb'), may hold values from -2 to 2
- bag_ids: int32 [800, 1024, 16], P('emb', 'rep'), may hold values from 0 to 1023
- bag_lengths: int32 [800, 1024], P('emb', 'rep'), may hold values from 1 to 16
- field_slot: int32 [800], replicated, may hold values from 0 to 799, each once
- pair_blocks: int32 [64, 2], replicated, may hold values from 0 to 99, as said below
- w_over: bfloat16 [4096, 4096], P(None, 'emb'), may hold values from -0.09375 to 0.09375
- b_over: bfloat16 [4096], P('emb'), may hold values from -3 to 3
- cotangent: bfloat16 [1024, 4096], P('rep', 'emb'), may hold values from -6 to 6
Outputs:
- over_out: bfloat16 [1024, 4096], P('rep', 'emb')
- grad_w: float32 [4096, 4096], P(None, 'emb')
- grad_b: float32 [4096], P('emb')
- pooled_grad: bfloat16 [800, 1024, 128], P('emb', 'rep')
Inputs may be any that keep to these rules, and one draw needn't show every extreme that they name: `pair_blocks`: each row names two field blocks, possibly equal; every block appears in some row.
All inputs are finite; a program needn't handle non-finite values.
Results may differ from a plain program's by a relative error of at most 0.0073.
Values may be sent and summed in bfloat16 or wider, within the bound.
A program may use at most 128 MiB of HBM per device.

v0:
```python
import functools
import math

import jax
import jax.numpy as jnp
from jax import lax
from jax.experimental import pallas as pl
from jax.experimental.pallas import tpu as pltpu
from jax.sharding import PartitionSpec as P

BLK = 8
NPAIR = 64
GROUP = 4
WORDS = 128
BITS = 4
NIBBLES = 0x0F0F0F0F


MESH = pl.DeviceIdType.MESH
TABLES = (5, 8, 8, 4)


def remote(src, dst, send_sem, recv_sem, device):
    return pltpu.make_async_remote_copy(
        src_ref=src,
        dst_ref=dst,
        send_sem=send_sem,
        recv_sem=recv_sem,
        device_id=device,
        device_id_type=MESH,
    )


def greet(devices):
    barrier = pltpu.get_barrier_semaphore()
    for device in devices:
        pl.semaphore_signal(barrier, inc=1, device_id=device, device_id_type=MESH)


def peer_order(ny, nx, ncore):
    left = [
        (dy, dx, dc)
        for dy in range(ny)
        for dx in range(nx)
        for dc in range(ncore)
        if (dy, dx, dc) != (0, 0, 0)
    ]

    def links(offset):
        used = []
        for axis, (step, size) in enumerate(((offset[0], ny), (offset[1], nx))):
            if 0 < step <= size // 2:
                used.append(2 * axis)
            if step >= size - size // 2 and step > 0:
                used.append(2 * axis + 1)
        return used

    order, load = [], [0] * 4

    def cost(offset):
        after = list(load)
        for link in links(offset):
            after[link] += 1
        return max(after) - min(after)

    while left:
        best = min(left, key=cost)
        left.remove(best)
        order.append(best)
        for link in links(best):
            load[link] += 1
    return order


def pooled_rows(ids, lengths, table):
    bag, samples = ids.shape
    used = lax.broadcasted_iota(jnp.int32, (bag, samples), 0) < lengths
    word = ids & (WORDS - 1)
    value = jnp.where(used, jnp.left_shift(1, (ids // WORDS) * BITS), 0)
    lows, highs = [], []
    for half in range(samples // 128):
        lanes = slice(half * 128, half * 128 + 128)
        row = lax.broadcasted_iota(jnp.int32, (WORDS, 128), 0)
        low, high = None, None
        for first in range(0, bag, 8):
            total = None
            for k in range(first, first + 8):
                hit = jnp.where(row == word[k : k + 1, lanes], value[k : k + 1, lanes], 0)
                total = hit if total is None else total + hit
            even, odd = total & NIBBLES, (total >> BITS) & NIBBLES
            low = even if low is None else low + even
            high = odd if high is None else high + odd
        lows.append(low)
        highs.append(high)
    bytes_of = [jnp.concatenate(lows, axis=1), jnp.concatenate(highs, axis=1)]
    chunks = []
    for part in range(table.shape[0] // WORDS):
        chunk = (bytes_of[part % 2] >> (8 * (part // 2))) & 31
        chunks.append(chunk.astype(jnp.float32).astype(jnp.bfloat16))
    pooled = lax.dot_general(
        table,
        jnp.concatenate(chunks, axis=0),
        (((0,), (0,)), ((), ())),
        preferred_element_type=jnp.float32,
    )
    return pooled.T.astype(jnp.bfloat16)


def group_masks(samples):
    n = GROUP * BLK * samples
    r = lax.broadcasted_iota(jnp.int32, (n, n), 0)
    c = lax.broadcasted_iota(jnp.int32, (n, n), 1)
    per = BLK * samples
    same = (r // per == c // per) & (r % samples == c % samples)
    return same


def select_matrix(samples, transposed):
    rows, cols = GROUP * BLK * samples, GROUP * BLK * BLK
    shape = (cols, rows) if transposed else (rows, cols)
    r = lax.broadcasted_iota(jnp.int32, shape, 1 if transposed else 0)
    c = lax.broadcasted_iota(jnp.int32, shape, 0 if transposed else 1)
    hit = (r // (BLK * samples) == c // (BLK * BLK)) & ((r // samples) % BLK == c % BLK)
    return jnp.where(hit, 1.0, 0.0).astype(jnp.bfloat16)


def own_columns(samples):
    rows, cols = GROUP * BLK * samples, GROUP * BLK * BLK
    r = lax.broadcasted_iota(jnp.int32, (rows, cols), 0)
    c = lax.broadcasted_iota(jnp.int32, (rows, cols), 1)
    return r // samples == c // BLK


STEP = 512


def scatter_index(pair_rows, slots):
    entries, nfields = 2 * pair_rows.shape[1], slots.shape[1]
    block = jnp.concatenate([pair_rows[0:1], pair_rows[1:2]], axis=1)
    square = (entries, entries)
    down = lax.broadcasted_iota(jnp.int32, square, 0)
    across = lax.broadcasted_iota(jnp.int32, square, 1)
    of_col = jnp.broadcast_to(block, square)
    of_row = of_col.T
    earlier = (of_row == of_col) & (down < across)
    rank = jnp.sum(jnp.where((of_row < of_col) | earlier, 1, 0), axis=0, keepdims=True)
    repeat = jnp.sum(jnp.where(earlier, 1, 0), axis=0, keepdims=True)
    hit = jnp.broadcast_to(rank, square).T == across
    order = jnp.sum(jnp.where(hit, down, 0), axis=0, keepdims=True)
    again = jnp.sum(jnp.where(hit, jnp.broadcast_to(repeat, square).T, 0), axis=0, keepdims=True)

    wide = (entries, nfields)
    own_block = lax.broadcasted_iota(jnp.int32, wide, 1) // BLK
    upto = jnp.where(of_row[:, :1] <= own_block, 1, 0)
    last = jnp.sum(upto, axis=0, keepdims=True) - 1
    piece = last * BLK + lax.broadcasted_iota(jnp.int32, (1, nfields), 1) % BLK
    places = []
    for start in range(0, nfields, entries):
        slot = lax.broadcasted_iota(jnp.int32, wide, 0) + start
        found = jnp.sum(jnp.where(slot == slots, piece, 0), axis=1, keepdims=True)
        row = jnp.broadcast_to(found, square).T
        places.append(jnp.clip(row[0:1], 0, entries * BLK - 1))
    return jnp.clip(order, 0, entries - 1), again, places


def step_kernel(
    slot_hbm,
    pair_hbm,
    ids_hbm,
    len_ref,
    tables_hbm,
    w_hbm,
    b_ref,
    cot_hbm,
    over_ref,
    gb_ref,
    out_ref,
    gall_ref,
    slot_ref,
    pair_ref,
    slot_row,
    pair_rows,
    index_rows,
    index_ref,
    fields_ref,
    dinter_ref,
    gw_ref,
    contrib,
    total_ref,
    back_ref,
    ids_ref,
    table_ref,
    rows_ref,
    pooled_ref,
    sel_ref,
    sel_t_ref,
    w_ref,
    cot_ref,
    gath,
    part,
    xrecv,
    sa,
    brecv,
    sb,
    crecv,
    gsend,
    grecv,
    bias,
    ag1_s,
    ag1_r,
    ag2_s,
    ag2_r,
    ag3_s,
    ag3_r,
    rs1_s,
    rs1_r,
    rs2_s,
    rs2_r,
    rs3_s,
    rs3_r,
    z_s,
    z_r,
    zb_s,
    zb_r,
    own_sem,
    table_sem,
    a2a_s,
    a2a_r,
    back_s,
    back_r,
    za_s,
    za_r,
):
    nhalf, ny, nx, ncore, per, width = gath.shape
    nrep = gsend.shape[0]
    samples = ny * nx * ncore * per
    hidden = w_ref.shape[1]
    rep, emb = lax.axis_index("rep"), lax.axis_index("emb")
    y, x, c = emb // (nx * ncore), lax.rem(emb // ncore, nx), lax.rem(emb, ncore)

    def at(yy, xx, cc):
        return (rep, (yy * nx + xx) * ncore + cc)

    xs = [lax.rem(x + k, nx) for k in range(nx)]
    ys = [lax.rem(y + k, ny) for k in range(ny)]
    zs = [lax.rem(rep + k, nrep) for k in range(nrep)]
    mate = at(y, x, 1 - c)
    peers = [
        at(ys[dy], xs[dx], lax.rem(c + dc, ncore)) for dy, dx, dc in peer_order(ny, nx, ncore)
    ]
    ndev, ntab, _, embed = rows_ref.shape
    nblocks = fields_ref.shape[0]

    get_ids = pltpu.make_async_copy(ids_hbm, ids_ref, own_sem.at[0])
    get_ids.start()
    small = [
        pltpu.make_async_copy(slot_hbm, slot_ref, own_sem.at[4]),
        pltpu.make_async_copy(pair_hbm, pair_ref, own_sem.at[5]),
        pltpu.make_async_copy(slot_hbm, slot_row.at[0], own_sem.at[6]),
        pltpu.make_async_copy(pair_hbm, pair_rows, own_sem.at[7]),
    ]
    for copy in small:
        copy.start()

    def get_tables(start, size, slot):
        return pltpu.make_async_copy(
            tables_hbm.at[pl.ds(start, size)],
            table_ref.at[slot, pl.ds(0, size)],
            table_sem.at[slot],
        )

    starts = [sum(TABLES[:n]) for n in range(len(TABLES))]
    for n in range(2):
        get_tables(starts[n], TABLES[n], n).start()
    get_w = pltpu.make_async_copy(w_hbm, w_ref, own_sem.at[1])
    get_w.start()
    get_cot = pltpu.make_async_copy(cot_hbm, cot_ref, own_sem.at[2])
    get_cot.start()
    greet(peers)
    greet([(zs[k], emb) for k in range(1, nrep)])
    get_ids.wait()

    def pool_tables(start, size, slot):
        for t in range(size):
            rows = pooled_rows(ids_ref[start + t], len_ref[pl.ds(start + t, 1)], table_ref[slot, t])
            rows_ref[:, start + t] = rows.reshape(ndev, per, embed)

    def send_rows(start, size):
        for _, peer in peers:
            remote(
                rows_ref.at[peer, pl.ds(start, size)],
                pooled_ref.at[pl.ds(emb * ntab + start, size)],
                a2a_s,
                a2a_r,
                (rep, peer),
            ).start()

    for n, size in enumerate(TABLES):
        get_tables(starts[n], size, n % 2).wait()
        pool_tables(starts[n], size, n % 2)
        if n + 2 < len(TABLES):
            get_tables(starts[n + 2], TABLES[n + 2], n % 2).start()
        if n == 0:
            pl.semaphore_wait(pltpu.get_barrier_semaphore(), ndev - 1 + nrep - 1)
        send_rows(starts[n], size)
    own_rows = pltpu.make_async_copy(
        rows_ref.at[emb], pooled_ref.at[pl.ds(emb * ntab, ntab)], own_sem.at[3]
    )
    own_rows.start()
    same = group_masks(per)
    own_cols = own_columns(per)
    sel_ref[...] = select_matrix(per, False)
    sel_t_ref[...] = select_matrix(per, True)
    for copy in small:
        copy.wait()
    order, again, place = scatter_index(pair_rows[...], slot_row[...])
    entries = order.shape[1]
    index_rows[0:1, 0:entries] = order
    index_rows[1:2, 0:entries] = again
    for n, row in enumerate(place):
        index_rows[2:3, n * entries : (n + 1) * entries] = row
    put_index = pltpu.make_async_copy(index_rows, index_ref, own_sem.at[8])
    put_index.start()
    own_rows.wait()
    others = pooled_ref.at[pl.ds(0, (ndev - 1) * ntab)]
    remote(others, others, a2a_s, a2a_r, mate).wait_recv()

    def gather(block, _):
        rows = [
            pooled_ref[slot_ref[block * BLK + i]].astype(jnp.float32) for i in range(BLK)
        ]
        fields_ref[block] = jnp.concatenate(rows, axis=0).astype(jnp.bfloat16)
        return 0

    lax.fori_loop(0, nblocks, gather, 0, unroll=4)

    sent = []

    def send(src, dst, send_sem, recv_sem, device, keep=True):
        copy = remote(src, dst, send_sem, recv_sem, device)
        copy.start()
        if keep:
            sent.append(copy)

    scale = 1.0 / math.sqrt(embed)
    group = GROUP * BLK * BLK
    own = [gath.at[half, y, x, c] for half in range(nhalf)]
    for half in range(nhalf):
        for q in range(width // group):
            first = half * (NPAIR // nhalf) + q * GROUP
            left = jnp.concatenate(
                [fields_ref[pair_ref[0, first + p]] for p in range(GROUP)], axis=0
            )
            right = jnp.concatenate(
                [fields_ref[pair_ref[1, first + p]] for p in range(GROUP)], axis=0
            )
            gram = lax.dot_general(
                left, right, (((1,), (1,)), ((), ())), preferred_element_type=jnp.float32
            )
            gram = jnp.where(same, gram * scale, 0.0).astype(jnp.bfloat16)
            spread = jnp.dot(gram, sel_ref[...], preferred_element_type=jnp.float32)
            kept = jnp.where(own_cols, spread, 0.0).reshape(GROUP * BLK, per, group)
            gath[half, y, x, c, :, q * group : (q + 1) * group] = jnp.sum(kept, axis=0).astype(
                jnp.bfloat16
            )
        for k in range(1, nx):
            near = at(y, xs[k], c) if half == 0 else at(ys[k], x, c)
            far = at(ys[k], x, c) if half == 0 else at(y, xs[k], c)
            send(own[half], own[half], ag1_s.at[half, k], ag1_r.at[half, k], near)
            send(own[half], own[half], ag2_s.at[half, k], ag2_r.at[half, k], far, False)
        send(own[half], own[half], ag3_s.at[half, 0], ag3_r.at[half, 0], mate, False)
    lines = [gath.at[0, y, :, c], gath.at[1, :, x, c]]
    for k in [1, nx - 1] + list(range(2, nx - 1)):
        for half in range(nhalf):
            block = gath.at[0, y, xs[nx - k], c] if half == 0 else gath.at[1, ys[ny - k], x, c]
            remote(block, block, ag1_s.at[half, k], ag1_r.at[half, k], mate).wait_recv()
            for j in range(1, nx):
                far = at(ys[j], x, c) if half == 0 else at(y, xs[j], c)
                send(block, block, ag2_s.at[half, j], ag2_r.at[half, j], far, False)
            send(block, block, ag3_s.at[half, 0], ag3_r.at[half, 0], mate, False)
    for k in [1, nx - 1] + list(range(2, nx - 1)):
        for half in range(nhalf):
            remote(lines[half], lines[half], ag2_s.at[half, k], ag2_r.at[half, k], mate).wait_recv()
            line = gath.at[0, ys[ny - k], :, c] if half == 0 else gath.at[1, :, xs[nx - k], c]
            send(line, line, ag3_s.at[half, k], ag3_r.at[half, k], mate)
    get_w.wait()
    get_cot.wait()
    steps = width // STEP
    pre = jnp.zeros((samples, hidden), jnp.float32)
    for half in range(nhalf):
        for k in range(nx):
            remote(lines[half], lines[half], ag3_s.at[half, k], ag3_r.at[half, k], mate).wait_recv()

        def forward(j, total):
            cols = pl.ds(pl.multiple_of(j * STEP, STEP), STEP)
            rows = pl.ds(pl.multiple_of(half * width + j * STEP, STEP), STEP)
            block = gath[half, :, :, :, :, cols].reshape(samples, STEP)
            return total + jnp.dot(block, w_ref[rows], preferred_element_type=jnp.float32)

        pre = lax.fori_loop(0, steps, forward, pre)
    pre = pre + b_ref[...].astype(jnp.float32)
    sig = jax.nn.sigmoid(pre)
    over_ref[...] = (pre * sig).astype(jnp.bfloat16)
    dpre = (cot_ref[...].astype(jnp.float32) * sig * (1.0 + pre * (1.0 - sig))).astype(jnp.bfloat16)

    for half in range(nhalf):

        def backward(j, _):
            cols = pl.ds(pl.multiple_of(j * STEP, STEP), STEP)
            rows = pl.ds(pl.multiple_of(half * width + j * STEP, STEP), STEP)
            block = lax.dot_general(
                dpre, w_ref[rows], (((1,), (1,)), ((), ())), preferred_element_type=jnp.float32
            )
            block = block.reshape(ny, nx, ncore, per, STEP)
            for core in range(ncore):
                part[half, core, :, :, :, cols] = block[:, :, core].astype(jnp.bfloat16)
            return 0

        lax.fori_loop(0, steps, backward, 0)
        send(part.at[half, 1 - c], xrecv.at[half], rs1_s.at[half], rs1_r.at[half], mate)

    later = [1, nx - 1] + list(range(2, nx - 1)) + [0]
    for half in range(nhalf):
        remote(xrecv.at[half], xrecv.at[half], rs1_s.at[half], rs1_r.at[half], mate).wait_recv()

        def add(j, _):
            sa[half, j] = (
                part[half, c, j].astype(jnp.float32) + xrecv[half, j].astype(jnp.float32)
            ).astype(jnp.bfloat16)
            return 0

        lax.fori_loop(0, ny, add, 0)
        for j in later:
            for k in range(1, nx):
                if half == 0:
                    src, device = sa.at[0, ys[k], xs[j]], at(ys[k], x, c)
                else:
                    src, device = sa.at[1, ys[j], xs[k]], at(y, xs[k], c)
                send(
                    src, brecv.at[half, k - 1, j], rs2_s.at[half, k, j], rs2_r.at[half, k, j], device
                )
    gb = jnp.sum(dpre.astype(jnp.float32), axis=0, keepdims=True)
    bias[rep] = jnp.broadcast_to(gb, bias.shape[1:])
    for k in range(1, nrep):
        send(bias.at[rep], bias.at[rep], zb_s.at[k], zb_r.at[k], (zs[k], emb))
    quarter = gsend.shape[1]
    for half in range(nhalf):

        def weights(j, _):
            cols = pl.ds(pl.multiple_of(j * STEP, STEP), STEP)
            block = gath[half, :, :, :, :, cols].reshape(samples, STEP)
            product = lax.dot_general(
                block, dpre, (((0,), (0,)), ((), ())), preferred_element_type=jnp.float32
            )
            place = half * (width // STEP) + j
            per_quarter = quarter // STEP
            rows = pl.ds(pl.multiple_of(lax.rem(place, per_quarter) * STEP, STEP), STEP)
            gsend[place // per_quarter, rows] = product.astype(jnp.bfloat16)
            return 0

        lax.fori_loop(0, steps, weights, 0)
    for k in range(1, nrep):
        send(gsend.at[zs[k]], grecv.at[k - 1], z_s.at[k], z_r.at[k], (zs[k], emb))

    for j in later:
        for half in range(nhalf):
            place = xs[j] if half == 0 else ys[j]
            mine = sa[0, y, place] if half == 0 else sa[1, place, x]
            total = mine.astype(jnp.float32)
            for k in range(1, nx):
                slot = brecv.at[half, k - 1, j]
                remote(slot, slot, rs2_s.at[half, k, j], rs2_r.at[half, k, j], mate).wait_recv()
                total = total + brecv[half, k - 1, j].astype(jnp.float32)
            sb[half, place] = total.astype(jnp.bfloat16)
            if j:
                device = at(y, xs[j], c) if half == 0 else at(ys[j], x, c)
                send(
                    sb.at[half, place],
                    crecv.at[half, j - 1],
                    rs3_s.at[half, j],
                    rs3_r.at[half, j],
                    device,
                )
    for half in range(nhalf):
        total = sb[half, x if half == 0 else y].astype(jnp.float32)
        for k in range(1, nx):
            slot = crecv.at[half, k - 1]
            remote(slot, slot, rs3_s.at[half, k], rs3_r.at[half, k], mate).wait_recv()
            total = total + crecv[half, k - 1].astype(jnp.float32)
        dinter_ref[:, half * width : (half + 1) * width] = total.astype(jnp.bfloat16)

    put_index.wait()
    for q in range(NPAIR // GROUP):
        left = jnp.concatenate(
            [fields_ref[pair_ref[0, q * GROUP + p]] for p in range(GROUP)], axis=0
        )
        right = jnp.concatenate(
            [fields_ref[pair_ref[1, q * GROUP + p]] for p in range(GROUP)], axis=0
        )
        entry = dinter_ref[:, q * group : (q + 1) * group].astype(jnp.float32)
        spread = jnp.broadcast_to(entry[None], (GROUP * BLK, per, group))
        spread = jnp.where(own_cols, spread.reshape(GROUP * BLK * per, group), 0.0)
        pair = jnp.dot(
            spread.astype(jnp.bfloat16), sel_t_ref[...], preferred_element_type=jnp.float32
        )
        pair = jnp.where(same, pair, 0.0).astype(jnp.bfloat16)
        to_left = jnp.dot(pair, right, preferred_element_type=jnp.float32) * scale
        to_right = (
            lax.dot_general(
                pair, left, (((0,), (0,)), ((), ())), preferred_element_type=jnp.float32
            )
            * scale
        )
        size = (GROUP, BLK * per, embed)
        contrib[q * GROUP : (q + 1) * GROUP] = to_left.reshape(size)
        contrib[NPAIR + q * GROUP : NPAIR + (q + 1) * GROUP] = to_right.reshape(size)

    def run(r, total):
        total = contrib[index_ref[0, r]] + jnp.where(index_ref[1, r] > 0, total, 0.0)
        total_ref[pl.ds(r * BLK, BLK)] = total.reshape(BLK, per, embed)
        return total

    lax.fori_loop(0, 2 * NPAIR, run, jnp.zeros((BLK * per, embed), jnp.float32), unroll=4)

    def fill(device):
        def one(t, _):
            back_ref[device, t] = total_ref[index_ref[2, device * ntab + t]].astype(jnp.bfloat16)
            return 0

        lax.fori_loop(0, ntab, one, 0, unroll=5)

    for _, peer in peers:
        fill(peer)
        remote(back_ref.at[peer], out_ref.at[emb], back_s, back_r, (rep, peer)).start()
    fill(emb)
    own_back = pltpu.make_async_copy(back_ref.at[emb], out_ref.at[emb], own_sem.at[9])
    own_back.start()

    for k in range(1, nrep):
        slot = grecv.at[k - 1]
        remote(slot, slot, z_s.at[k], z_r.at[k], mate).wait_recv()
        remote(bias.at[rep], bias.at[rep], zb_s.at[k], zb_r.at[k], mate).wait_recv()
    total = gsend[rep].astype(jnp.float32)
    for k in range(1, nrep):
        total = total + grecv[k - 1].astype(jnp.float32)
    gw_ref[...] = total.astype(jnp.bfloat16)
    for k in range(1, nrep):
        send(gw_ref, gall_ref.at[rep], za_s.at[k], za_r.at[k], (zs[k], emb))
    own_gw = pltpu.make_async_copy(gw_ref, gall_ref.at[rep], own_sem.at[10])
    own_gw.start()
    gb_ref[...] = jnp.sum(bias[...], axis=0)[:1]

    own_back.wait()
    own_gw.wait()
    for k in range(1, nrep):
        remote(gw_ref, gall_ref.at[0], za_s.at[k], za_r.at[k], mate).wait_recv()
    others = out_ref.at[pl.ds(0, ndev - 1)]
    remote(others, others, back_s, back_r, mate).wait_recv()
    sources = rows_ref.at[pl.ds(0, ndev - 1)]
    remote(sources, sources, a2a_s, a2a_r, mate).wait_send()
    sources = back_ref.at[pl.ds(0, ndev - 1)]
    remote(sources, sources, back_s, back_r, mate).wait_send()
    for half in range(nhalf):
        line = lines[half]
        for k in range(1, nx):
            remote(line, line, ag2_s.at[half, k], ag2_r.at[half, k], mate).wait_send()
        remote(line, line, ag3_s.at[half, 0], ag3_r.at[half, 0], mate).wait_send()
    for copy in sent:
        copy.wait_send()


def train_step(ids, lengths, tables, field_slot, pairs, w, b, cot, grid):
    nrep, ny, nx, ncore = grid
    ndev = ny * nx * ncore
    ntab, bag, samples = ids.shape
    rows, embed = tables.shape[1:]
    per = samples // ndev
    features, hidden = w.shape
    nblocks = ndev * ntab // BLK
    nhalf, width, quarter = 2, features // 2, features // nrep
    half_rows = (nhalf, ny, nx, per, width)
    group = GROUP * BLK * BLK
    dma = pltpu.SemaphoreType.DMA
    bf16 = jnp.bfloat16
    vmem = pl.BlockSpec(memory_space=pltpu.VMEM)
    anywhere = pl.BlockSpec(memory_space=pl.ANY)
    return pl.pallas_call(
        step_kernel,
        in_specs=[anywhere, anywhere, anywhere, vmem, anywhere, anywhere, vmem, anywhere],
        out_specs=[vmem, vmem, anywhere, anywhere],
        out_shape=[
            jax.ShapeDtypeStruct((samples, hidden), bf16),
            jax.ShapeDtypeStruct((1, hidden), jnp.float32),
            jax.ShapeDtypeStruct((ndev, ntab, per, embed), bf16),
            jax.ShapeDtypeStruct((nrep, quarter, hidden), bf16),
        ],
        scratch_shapes=[
            pltpu.SMEM((ndev * ntab,), jnp.int32),
            pltpu.SMEM(pairs.shape, jnp.int32),
            pltpu.VMEM((1, ndev * ntab), jnp.int32),
            pltpu.VMEM(pairs.shape, jnp.int32),
            pltpu.VMEM((8, 1024), jnp.int32),
            pltpu.SMEM((8, 1024), jnp.int32),
            pltpu.VMEM((nblocks, BLK * per, embed), bf16),
            pltpu.VMEM((per, features), bf16),
            pltpu.VMEM((quarter, hidden), bf16),
            pltpu.VMEM((2 * NPAIR, BLK * per, embed), jnp.float32),
            pltpu.VMEM((2 * NPAIR * BLK, per, embed), jnp.float32),
            pltpu.VMEM((ndev, ntab, per, embed), bf16),
            pltpu.VMEM((ntab, bag, samples), jnp.int32),
            pltpu.VMEM((2, max(TABLES), rows, embed), bf16),
            pltpu.VMEM((ndev, ntab, per, embed), bf16),
            pltpu.VMEM((ndev * ntab, per, embed), bf16),
            pltpu.VMEM((group, group), bf16),
            pltpu.VMEM((group, group), bf16),
            pltpu.VMEM((features, hidden), bf16),
            pltpu.VMEM((samples, hidden), bf16),
            pltpu.VMEM((nhalf, ny, nx, ncore, per, width), bf16),
            pltpu.VMEM((nhalf, ncore, ny, nx, per, width), bf16),
            pltpu.VMEM(half_rows, bf16),
            pltpu.VMEM(half_rows, bf16),
            pltpu.VMEM((nhalf, nx - 1, nx, per, width), bf16),
            pltpu.VMEM((nhalf, nx, per, width), bf16),
            pltpu.VMEM((nhalf, nx - 1, per, width), bf16),
            pltpu.VMEM((nrep, quarter, hidden), bf16),
            pltpu.VMEM((nrep - 1, quarter, hidden), bf16),
            pltpu.VMEM((nrep, 8, hidden), jnp.float32),
        ]
        + [dma((nhalf, nx))] * 6
        + [dma((nhalf,))] * 2
        + [dma((nhalf, nx, nx))] * 2
        + [dma((nhalf, nx))] * 2
        + [dma((nrep,))] * 4
        + [dma((11,)), dma((2,)), dma, dma, dma, dma, dma((nrep,)), dma((nrep,))],
        compiler_params=pltpu.CompilerParams(
            vmem_limit_bytes=60 << 20, collective_id=0, has_side_effects=True
        ),
        name="train_step",
    )(
        field_slot,
        pairs,
        ids,
        lengths,
        tables,
        w,
        b.reshape(1, hidden),
        cot,
    )


PARTS = 4


def finish_kernel(
    rows_ref,
    gall_ref,
    over_ref,
    gb_ref,
    pooled_out,
    gw_out,
    over_out,
    gb_out,
    held,
    half,
    full,
    small,
    tiny,
    sems,
):
    nrep, quarter = gall_ref.shape[:2]
    ndev = rows_ref.shape[0]
    size = ndev // PARTS
    first = [pltpu.make_async_copy(gall_ref.at[q], half.at[q], sems.at[0, q]) for q in range(nrep)]
    rows = [
        pltpu.make_async_copy(
            rows_ref.at[pl.ds(g * size, size)], held.at[pl.ds(g * size, size)], sems.at[1, g]
        )
        for g in range(PARTS)
    ]
    extra = [
        pltpu.make_async_copy(over_ref, small, sems.at[4, 0]),
        pltpu.make_async_copy(gb_ref, tiny, sems.at[4, 1]),
    ]
    for copy in [copy for two in zip(rows, first) for copy in two] + extra:
        copy.start()
    out = []
    for g in range(PARTS):
        rows[g].wait()
        for d in range(g * size, (g + 1) * size):
            pltpu.make_async_copy(held.at[d], pooled_out.at[:, d], sems.at[2, 0]).start()
        first[g].wait()
        full[g] = half[g].astype(jnp.float32)
        copy = pltpu.make_async_copy(
            full.at[g], gw_out.at[pl.ds(g * quarter, quarter)], sems.at[3, g]
        )
        copy.start()
        out.append(copy)
    for copy in extra:
        copy.wait()
    last = [
        pltpu.make_async_copy(small, over_out, sems.at[4, 2]),
        pltpu.make_async_copy(tiny, gb_out, sems.at[4, 3]),
    ]
    for copy in last:
        copy.start()
    for copy in last + out:
        copy.wait()
    pltpu.make_async_copy(pooled_out, pooled_out, sems.at[2, 0]).wait()


def finish(rows, gw_all, over, gb):
    ndev, ntab, per, embed = rows.shape
    nrep, quarter, hidden = gw_all.shape
    anywhere = pl.BlockSpec(memory_space=pl.ANY)
    return pl.pallas_call(
        finish_kernel,
        in_specs=[anywhere] * 4,
        out_specs=[anywhere] * 4,
        out_shape=[
            jax.ShapeDtypeStruct((ntab, ndev, per, embed), rows.dtype),
            jax.ShapeDtypeStruct((nrep * quarter, hidden), jnp.float32),
            jax.ShapeDtypeStruct(over.shape, over.dtype),
            jax.ShapeDtypeStruct(gb.shape, gb.dtype),
        ],
        scratch_shapes=[
            pltpu.VMEM(rows.shape, rows.dtype),
            pltpu.VMEM(gw_all.shape, gw_all.dtype),
            pltpu.VMEM(gw_all.shape, jnp.float32),
            pltpu.VMEM(over.shape, over.dtype),
            pltpu.VMEM(gb.shape, gb.dtype),
            pltpu.SemaphoreType.DMA((5, nrep)),
        ],
        compiler_params=pltpu.CompilerParams(vmem_limit_bytes=60 << 20),
        name="finish",
    )(rows, gw_all, over, gb)


def on_device(tables, bag_ids, bag_lengths, field_slot, pair_blocks, w_over, b_over, cotangent):
    grid = (lax.axis_size("rep"), 4, 4, 2)
    ids, pairs = jnp.swapaxes(bag_ids, 1, 2), pair_blocks.T
    over, gb, rows, gw_all = train_step(
        ids, bag_lengths, tables, field_slot, pairs, w_over, b_over, cotangent, grid
    )
    pooled_grad, grad_w, over_out, grad_b = finish(rows, gw_all, over, gb)
    return (
        over_out,
        grad_w,
        grad_b.reshape(b_over.shape),
        pooled_grad.reshape(tables.shape[0], bag_ids.shape[1], tables.shape[2]),
    )


def solution(mesh):
    in_specs = (
        P("emb", None, None),
        P("emb", "rep", None),
        P("emb", "rep"),
        P(),
        P(),
        P(None, "emb"),
        P("emb"),
        P("rep", "emb"),
    )
    out_specs = (P("rep", "emb"), P(None, "emb"), P("emb"), P("emb", "rep", None))
    return jax.shard_map(
        on_device, mesh=mesh, in_specs=in_specs, out_specs=out_specs, check_vma=False
    )
```

profile of v0, /device:TPU:1, one launch (start us, length us, event | category | flops | bytes accessed | tf_op | source)
XLA Modules:
  0.0 88.3 jit_solution(11094969435624857942)
XLA Ops:
  0.6 84.4 %train_step.1 = (bf16[256,128]{1,0:T(8,128)(2,1)}, f32[1,128]{1,0:T(1,128)}, bf16[32,25,8,128]{3,2,1,0:T(8,128)(2,1)}, bf16[4,1024,128]{2,1,0:T(8,128)(2,1)}) custom-call(s32[800]{0:T(1024)} %slot_hbm.1, s32[2,64]{1,0:T(2,128)} %bitcast.6, s32[25,16,256]{2,1,0:T(8,128)} %bitcast.5, s32[25,256]{1,0:T(8,128)} %len_ref.1, bf16[25,1024,128]{2,1,0:T(8,128)(2,1)} %tables_hbm.1, ...), custom_call_target="tpu_custom_call" | custom-call | tf_op jit(solution)/shard_map/train_step/pallas_call | solution.py:587
  85.1 3.0 %finish.1 = (bf16[25,32,8,128]{3,2,1,0:T(8,128)(2,1)}, f32[4096,128]{1,0:T(8,128)}, bf16[256,128]{1,0:T(8,128)(2,1)}, f32[1,128]{1,0:T(1,128)}) custom-call(bf16[32,25,8,128]{3,2,1,0:T(8,128)(2,1)} %get-tuple-element.12.rows_ref, bf16[4,1024,128]{2,1,0:T(8,128)(2,1)} %get-tuple-element.13.gall_ref, bf16[256,128]{1,0:T(8,128)(2,1)} %get-tuple-element.14.over_ref, ...), custom_call_target="tpu_custom_call" | custom-call | tf_op jit(solution)/shard_map/finish/pallas_call | solution.py:715
where the time goes:
time: 88.5 us; the launch traced here: 88.3 us
  Pallas kernels  87.5 us (99%)
    pallas_call x1, Pallas kernels, train_step(): pl.pallas_call(step_kernel, in_specs=[anywhere, anywhere, anywhere, vmem,...  84.4 us
    pallas_call x1, Pallas kernels, finish(): pl.pallas_call(finish_kernel, in_specs=[anywhere] * 4, out_specs=[anywher...  3.05 us

commit v1 on v0

--- a/solution.py
+++ b/solution.py
@@ -17,7 +17,7 @@
 
 
 MESH = pl.DeviceIdType.MESH
-TABLES = (5, 8, 8, 4)
+TABLES = (6, 8, 7, 4)
 
 
 def remote(src, dst, send_sem, recv_sem, device):
@@ -529,25 +529,30 @@
 
         lax.fori_loop(0, ntab, one, 0, unroll=5)
 
-    for _, peer in peers:
+    def gather_weights():
+        for k in range(1, nrep):
+            slot = grecv.at[k - 1]
+            remote(slot, slot, z_s.at[k], z_r.at[k], mate).wait_recv()
+            remote(bias.at[rep], bias.at[rep], zb_s.at[k], zb_r.at[k], mate).wait_recv()
+        total = gsend[rep].astype(jnp.float32)
+        for k in range(1, nrep):
+            total = total + grecv[k - 1].astype(jnp.float32)
+        gw_ref[...] = total.astype(jnp.bfloat16)
+        for k in range(1, nrep):
+            send(gw_ref, gall_ref.at[rep], za_s.at[k], za_r.at[k], (zs[k], emb))
+        own_gw = pltpu.make_async_copy(gw_ref, gall_ref.at[rep], own_sem.at[10])
+        own_gw.start()
+        return own_gw
+
+    for n, (_, peer) in enumerate(peers):
+        if n == 8:
+            own_gw = gather_weights()
         fill(peer)
         remote(back_ref.at[peer], out_ref.at[emb], back_s, back_r, (rep, peer)).start()
     fill(emb)
     own_back = pltpu.make_async_copy(back_ref.at[emb], out_ref.at[emb], own_sem.at[9])
     own_back.start()
 
-    for k in range(1, nrep):
-        slot = grecv.at[k - 1]
-        remote(slot, slot, z_s.at[k], z_r.at[k], mate).wait_recv()
-        remote(bias.at[rep], bias.at[rep], zb_s.at[k], zb_r.at[k], mate).wait_recv()
-    total = gsend[rep].astype(jnp.float32)
-    for k in range(1, nrep):
-        total = total + grecv[k - 1].astype(jnp.float32)
-    gw_ref[...] = total.astype(jnp.bfloat16)
-    for k in range(1, nrep):
-        send(gw_ref, gall_ref.at[rep], za_s.at[k], za_r.at[k], (zs[k], emb))
-    own_gw = pltpu.make_async_copy(gw_ref, gall_ref.at[rep], own_sem.at[10])
-    own_gw.start()
     gb_ref[...] = jnp.sum(bias[...], axis=0)[:1]
 
     own_back.wait()

time: 88.5 us -> 88.8 us (level)
  no operation moved by 1% of the time
where the time goes in v1:
time: 88.8 us; the launch traced here: 88.6 us
  Pallas kernels  87.8 us (99%)
    pallas_call x1, Pallas kernels, train_step(): pl.pallas_call(step_kernel, in_specs=[anywhere, anywhere, anywhere, vmem,...  84.8 us
    pallas_call x1, Pallas kernels, finish(): pl.pallas_call(finish_kernel, in_specs=[anywhere] * 4, out_specs=[anywher...  3.05 us

profile of v1, /device:TPU:1, one launch (start us, length us, event | category | flops | bytes accessed | tf_op | source)
XLA Modules:
  0.0 88.6 jit_solution(6045114864214629155)
XLA Ops:
  0.6 84.8 %train_step.1 = (bf16[256,128]{1,0:T(8,128)(2,1)}, f32[1,128]{1,0:T(1,128)}, bf16[32,25,8,128]{3,2,1,0:T(8,128)(2,1)}, bf16[4,1024,128]{2,1,0:T(8,128)(2,1)}) custom-call(s32[800]{0:T(1024)} %slot_hbm.1, s32[2,64]{1,0:T(2,128)} %bitcast.6, s32[25,16,256]{2,1,0:T(8,128)} %bitcast.5, s32[25,256]{1,0:T(8,128)} %len_ref.1, bf16[25,1024,128]{2,1,0:T(8,128)(2,1)} %tables_hbm.1, ...), custom_call_target="tpu_custom_call" | custom-call | tf_op jit(solution)/shard_map/train_step/pallas_call | solution.py:592
  85.4 3.0 %finish.1 = (bf16[25,32,8,128]{3,2,1,0:T(8,128)(2,1)}, f32[4096,128]{1,0:T(8,128)}, bf16[256,128]{1,0:T(8,128)(2,1)}, f32[1,128]{1,0:T(1,128)}) custom-call(bf16[32,25,8,128]{3,2,1,0:T(8,128)(2,1)} %get-tuple-element.12.rows_ref, bf16[4,1024,128]{2,1,0:T(8,128)(2,1)} %get-tuple-element.13.gall_ref, bf16[256,128]{1,0:T(8,128)(2,1)} %get-tuple-element.14.over_ref, ...), custom_call_target="tpu_custom_call" | custom-call | tf_op jit(solution)/shard_map/finish/pallas_call | solution.py:720
